TPU v7x, 32 devices: a whole 2x2x4 slice. The times are simulated.
32 devices in a mesh: cohort: 2 (over x), grp: 4 (over z), vox: 4 (over y, core).
Axes of the slice: x: 2, y: 2, z: 4, core: 2. Of those that a mesh axis runs over, the one named last changes fastest.
Arguments:
- probes: bfloat16 [16384, 256], P(('cohort', 'grp', 'vox')), parts along dimension 0, may hold values from -6 to 6
- blocks: bfloat16 [512, 4, 128, 128], P(('cohort', 'grp', 'vox')), parts along dimension 0, may hold values from -0.25 to 0.25
- pattern: int32 [512, 4], P(('cohort', 'grp', 'vox')), parts along dimension 0, may hold values from 0 to 31, as said below
- scale_exp: int32 [512, 4], P(('cohort', 'grp', 'vox')), parts along dimension 0, may hold values from -2 to 2
- noise: float32 [512, 128], P(('cohort', 'grp', 'vox')), parts along dimension 0, may hold values from 0.1 to 1
Outputs:
- hessian_probes: float32 [16384, 256], P(('cohort', 'grp', 'vox')), parts along dimension 0
There are 2 independent parts, one for each index of `cohort`. A program takes and returns all parts, laid end to end along the dimension named above; each array names one. Nothing has to cross between parts.
Inputs may be any that keep to these rules, and one draw needn't show every extreme that they name: pattern is below 16 in the last group's rows; other rows may reach into the next group's parameter blocks.
All inputs are finite; a program needn't handle non-finite values.
Results may differ from a plain program's by a relative error of at most 0.0016.
Values may be sent and summed in bfloat16 or wider, within the bound.
A program may use at most 128 MiB of HBM per device.

v0:
```python
import jax
import jax.numpy as jnp
from jax import lax
from jax.sharding import PartitionSpec as P


def shifted(array, axis, by):
    devices = lax.axis_size(axis)
    pairs = [(i, i + by) for i in range(devices) if 0 <= i + by < devices]
    return lax.ppermute(array, axis, pairs)


def local(probes, blocks, pattern, scale_exp, noise):
    rows_here = blocks.shape[0]
    width = blocks.shape[2]
    count = blocks.shape[1]
    probe_cols = probes.shape[1]
    own_panel = lax.all_gather(probes, "vox", axis=0, tiled=True)
    next_rows = shifted(own_panel, "grp", -1)
    group_rows = own_panel.shape[0] // width
    panels = jnp.concatenate([own_panel, next_rows], axis=0).reshape(
        2 * group_rows, width, probe_cols
    )
    scales = jnp.exp2(scale_exp.astype(jnp.float32))
    forward = jnp.zeros((rows_here, width, probe_cols), jnp.float32)
    for slot in range(count):
        picked = panels[pattern[:, slot]]
        product = jnp.einsum(
            "rab,rbk->rak", blocks[:, slot], picked, preferred_element_type=jnp.float32
        )
        forward = forward + product * scales[:, slot, None, None]
    weighted = (noise[:, :, None] * forward).astype(jnp.bfloat16)
    partial_value = jnp.zeros((2 * group_rows, width, probe_cols), jnp.float32)
    for slot in range(count):
        back = jnp.einsum(
            "rab,rak->rbk", blocks[:, slot], weighted, preferred_element_type=jnp.float32
        )
        partial_value = partial_value.at[pattern[:, slot]].add(back * scales[:, slot, None, None])
    own_part = partial_value[:group_rows].reshape(group_rows * width, probe_cols)
    next_part = partial_value[group_rows:].reshape(group_rows * width, probe_cols)
    mine, theirs = (
        lax.psum_scatter(own_part, "vox", scatter_dimension=0, tiled=True),
        lax.psum_scatter(next_part, "vox", scatter_dimension=0, tiled=True),
    )
    result = mine + shifted(theirs, "grp", 1)
    return result


def solution(mesh):
    in_specs = (
        P(("cohort", "grp", "vox"), None),
        P(("cohort", "grp", "vox"), None, None, None),
        P(("cohort", "grp", "vox"), None),
        P(("cohort", "grp", "vox"), None),
        P(("cohort", "grp", "vox"), None),
    )
    out_specs = P(("cohort", "grp", "vox"), None)
    return jax.shard_map(local, mesh=mesh, in_specs=in_specs, out_specs=out_specs, check_vma=False)
```

profile of v0, /device:TPU:0, one launch (start us, length us, event | category | flops | bytes accessed | tf_op | source)
XLA Modules:
  0.0 188.6 jit_solution(3924717938640009242)
XLA Ops:
  7.3 21.1 %all-gather.2.cloned.1.call-done = bf16[2048,256]{1,0:T(8,128)(2,1)} async-done(((bf16[512,256]{1,0:T(8,128)(2,1)}), bf16[2048,256]{1,0:T(8,128)(2,1)}) %all-gather.2.cloned.1.call-update) | async-done | bytes 1048592 | tf_op jit(solution)/shard_map/all_gather | solution.py:18
  31.2 24.5 %collective-permute-done = bf16[2048,256]{1,0:T(8,128)(2,1)S(1)} collective-permute-done((bf16[2048,256]{1,0:T(8,128)(2,1)}, bf16[2048,256]{1,0:T(8,128)(2,1)S(1)}, u32[]{:S(2)}, u32[]{:S(2)}) %collective-permute-start) | collective-permute-done | bytes 1048608 | tf_op jit(solution)/shard_map/ppermute | solution.py:10
  57.8 1.6 gather_fusion.1
  59.4 3.0 %fusion.3 = f32[16,256,128]{2,1,0:T(8,128)} fusion(bf16[16,128,256]{2,1,0:T(8,128)(2,1)S(1)} %gather_fusion.2, bf16[16,4,128,128]{3,2,1,0:T(8,128)(2,1)} %param.6), kind=kOutput, calls=%fused_computation.17 | convolution fusion | flops 134217728 | bytes 3670016 | tf_op jit(solution)/shard_map/rab,rbk->rak/dot_general | solution.py:28
  62.3 2.8 %fusion.6 = f32[16,256,128]{2,1,0:T(8,128)} fusion(bf16[16,128,256]{2,1,0:T(8,128)(2,1)S(1)} %copy-done.2, bf16[16,4,128,128]{3,2,1,0:T(8,128)(2,1)} %param.6), kind=kOutput, calls=%fused_computation.20 | convolution fusion | flops 134217728 | bytes 3670016 | tf_op jit(solution)/shard_map/rab,rbk->rak/dot_general | solution.py:28
  65.8 2.8 %fusion.9 = f32[16,256,128]{2,1,0:T(8,128)} fusion(bf16[16,128,256]{2,1,0:T(8,128)(2,1)S(1)} %gather_fusion, bf16[16,4,128,128]{3,2,1,0:T(8,128)(2,1)} %param.6), kind=kOutput, calls=%fused_computation.23 | convolution fusion | flops 134217728 | bytes 3670016 | tf_op jit(solution)/shard_map/rab,rbk->rak/dot_general | solution.py:28
  69.3 4.2 %multiply_convert_fusion = bf16[16,256,128]{2,1,0:T(8,128)(2,1)S(1)} fusion(f32[16,256,128]{2,1,0:T(8,128)} %fusion.3, f32[16,256,128]{2,1,0:T(8,128)} %fusion.6, f32[16,256,128]{2,1,0:T(8,128)} %fusion.9, bf16[16,128,256]{2,1,0:T(8,128)(2,1)S(1)} %gather_fusion.3, f32[16,128]{1,0:T(8,128)S(1)} %copy-done.3, f32[16]{0:T(128)S(1)} %get-tuple-element.8, ...), kind=kOutput, calls=%fused_computation.9 | convolution fusion | flops 138936320 | bytes 8921344 | tf_op jit(solution)/shard_map/rab,rbk->rak/dot_general | solution.py:28
  73.9 1.7 multiply_bitcast_fusion.2
  75.7 1.8 multiply_bitcast_fusion.1
  77.4 1.8 multiply_bitcast_fusion
  79.2 1.9 copy.22
  81.1 3.1 %copy.23 = f32[16,128,256]{2,1,0:T(8,128)} copy(f32[16,128,256]{1,2,0:T(8,128)} %multiply_bitcast_fusion.2) | data formatting | bytes 4194304 | tf_op jit(solution)/shard_map/mul | solution.py:38
  84.1 1.8 copy.24
  86.0 1.9 %copy.25 = f32[16,128,256]{2,1,0:T(8,128)S(1)} copy(f32[16,128,256]{1,2,0:T(8,128)} %multiply_bitcast_fusion) | data formatting | bytes 4194304 | tf_op jit(solution)/shard_map/mul | solution.py:38
  87.9 2.4 %broadcast_in_dim.2 = f32[32,128,256]{2,1,0:T(8,128)} broadcast(f32[]{:T(128)} %constant.0.clone.1), dimensions={} | broadcast | bytes 4194308 | tf_op jit(solution)/shard_map/broadcast_in_dim | solution.py:33
  90.3 5.3 %scatter_fusion = f32[32,128,256]{2,1,0:T(8,128)} fusion(f32[32,128,256]{2,1,0:T(8,128)} %broadcast_in_dim.2, s32[16]{0:T(128)S(1)} %get-tuple-element.13, f32[16,128,256]{2,1,0:T(8,128)} %copy.22), kind=kCustom, calls=%fused_computation.4 | custom fusion | flops 524288 | bytes 6291520 | tf_op jit(solution)/shard_map/scatter-add | solution.py:38
  95.6 5.3 %scatter_fusion.1 = f32[32,128,256]{2,1,0:T(8,128)} fusion(f32[32,128,256]{2,1,0:T(8,128)} %scatter_fusion, s32[16]{0:T(128)S(1)} %get-tuple-element.12, f32[16,128,256]{2,1,0:T(8,128)} %copy.23), kind=kCustom, calls=%fused_computation.5 | custom fusion | flops 524288 | bytes 6291520 | tf_op jit(solution)/shard_map/scatter-add | solution.py:38
  100.8 5.2 %scatter_fusion.2 = f32[32,128,256]{2,1,0:T(8,128)} fusion(f32[32,128,256]{2,1,0:T(8,128)} %scatter_fusion.1, s32[16]{0:T(128)S(1)} %get-tuple-element.14, f32[16,128,256]{2,1,0:T(8,128)} %copy.24), kind=kCustom, calls=%fused_computation.6 | custom fusion | flops 524288 | bytes 6291520 | tf_op jit(solution)/shard_map/scatter-add | solution.py:38
  106.1 4.5 %scatter_fusion.3 = f32[32,128,256]{2,1,0:T(8,128)} fusion(f32[32,128,256]{2,1,0:T(8,128)} %scatter_fusion.2, s32[16]{0:T(128)S(1)} %get-tuple-element.11, f32[16,128,256]{2,1,0:T(8,128)S(1)} %copy.25), kind=kCustom, calls=%fused_computation.7 | custom fusion | flops 524288 | bytes 6291520 | tf_op jit(solution)/shard_map/scatter-add | solution.py:38
  110.6 4.7 %fusion.23 = (f32[16,128,256]{2,1,0:T(8,128)}, f32[16,128,256]{2,1,0:T(8,128)}) fusion(f32[32,128,256]{2,1,0:T(8,128)} %scatter_fusion.3), kind=kLoop, calls=%fused_computation.50 | loop fusion | bytes 8388608 | tf_op jit(solution)/shard_map/slice | solution.py:40
  116.0 30.0 %reduce-scatter.5.cloned.1.call-done = f32[512,256]{1,0:T(8,128)} async-done(((f32[2048,256]{1,0:T(8,128)}), f32[512,256]{1,0:T(8,128)}) %reduce-scatter.5.cloned.1.call-update) | async-done | bytes 524304 | tf_op jit(solution)/shard_map/reduce_scatter | solution.py:43
  146.0 3.4 %collective-permute-start.1 = (f32[512,256]{1,0:T(8,128)}, f32[512,256]{1,0:T(8,128)S(1)}, u32[]{:S(2)}, u32[]{:S(2)}) collective-permute-start(f32[512,256]{1,0:T(8,128)} %reduce-scatter.5.cloned.1.call-done), channel_id=1, source_target_pairs={{0,4},{4,8},{8,12},{1,5},{5,9},{9,13},{2,6},{6,10},{10,14},{3,7},{... | collective-permute-start | bytes 1572872 | tf_op jit(solution)/shard_map/ppermute | solution.py:10
  149.4 30.8 %reduce-scatter.3.cloned.1.call-done = f32[512,256]{1,0:T(8,128)} async-done(((f32[2048,256]{1,0:T(8,128)}), f32[512,256]{1,0:T(8,128)}) %reduce-scatter.3.cloned.1.call-update) | async-done | bytes 524304 | tf_op jit(solution)/shard_map/reduce_scatter | solution.py:42
  180.1 1.9 %add.57 = f32[512,256]{1,0:T(8,128)} add(f32[512,256]{1,0:T(8,128)} %reduce-scatter.3.cloned.1.call-done, f32[512,256]{1,0:T(8,128)S(1)} %collective-permute-done.1) | non-fusion elementwise | flops 131072 | bytes 1572864 | tf_op jit(solution)/shard_map/add | solution.py:45
  (26 shorter events, 8.0 us)
Async XLA Ops:
  6.5 21.8 %all-gather.2.cloned.1.call-start = ((), (), s32[]{:S(2)}) async-start(), calls=%async_computation.2 | async-start | bytes 1310720 | tf_op jit(solution)/shard_map/all_gather | solution.py:18
  7.3 138.7 %reduce-scatter.5.cloned.1.call-start = ((), (), s32[]{:S(2)}) async-start(), calls=%async_computation.4 | async-start | bytes 2621440 | tf_op jit(solution)/shard_map/reduce_scatter | solution.py:43
  28.4 27.4 %collective-permute-start = (bf16[2048,256]{1,0:T(8,128)(2,1)}, bf16[2048,256]{1,0:T(8,128)(2,1)S(1)}, u32[]{:S(2)}, u32[]{:S(2)}) collective-permute-start(bf16[2048,256]{1,0:T(8,128)(2,1)} %all-gather.2.cloned.1.call-done), channel_id=1, source_target_pairs={{4,0},{8,4},{12,8},{5,1},{9,5},{13,9},{6,2},{10,6},{14,10},{7,3},{... | collective-permute-start | bytes 3145736 | tf_op jit(solution)/shard_map/ppermute | solution.py:10
  59.4 3.0 %copy-start.2 = (bf16[16,128,256]{2,1,0:T(8,128)(2,1)S(1)}, bf16[16,128,256]{2,1,0:T(8,128)(2,1)}, u32[]{:S(2)}) copy-start(bf16[16,128,256]{2,1,0:T(8,128)(2,1)} %gather_fusion.1) | copy-start | bytes 3145732
  65.8 3.5 %copy-start.3 = (f32[16,128]{1,0:T(8,128)S(1)}, f32[16,128]{1,0:T(8,128)}, u32[]{:S(2)}) copy-start(f32[16,128]{1,0:T(8,128)} %param.9) | copy-start | bytes 24580
  69.3 4.2 %copy-start = (bf16[16,4,128,128]{3,2,1,0:T(8,128)(2,1)S(1)}, bf16[16,4,128,128]{3,2,1,0:T(8,128)(2,1)}, u32[]{:S(2)}) copy-start(bf16[16,4,128,128]{3,2,1,0:T(8,128)(2,1)} %param.6) | copy-start | bytes 6291460
  81.1 3.1 %copy-start.1 = (f32[16,128,256]{1,2,0:T(8,128)S(1)}, f32[16,128,256]{1,2,0:T(8,128)}, u32[]{:S(2)}) copy-start(f32[16,128,256]{1,2,0:T(8,128)} %multiply_bitcast_fusion.1) | copy-start | bytes 6291460
  115.2 64.9 %reduce-scatter.3.cloned.1.call-start = ((), (), s32[]{:S(2)}) async-start(), calls=%async_computation.3 | async-start | bytes 2621440 | tf_op jit(solution)/shard_map/reduce_scatter | solution.py:42
  146.0 34.2 %collective-permute-start.1 = (f32[512,256]{1,0:T(8,128)}, f32[512,256]{1,0:T(8,128)S(1)}, u32[]{:S(2)}, u32[]{:S(2)}) collective-permute-start(f32[512,256]{1,0:T(8,128)} %reduce-scatter.5.cloned.1.call-done), channel_id=1, source_target_pairs={{0,4},{4,8},{8,12},{1,5},{5,9},{9,13},{2,6},{6,10},{10,14},{3,7},{... | collective-permute-start | bytes 1572872 | tf_op jit(solution)/shard_map/ppermute | solution.py:10
Sparse Core Ops, SparseCore 0:
  8.9 19.4 all-gather.1
  115.4 30.5 reduce-scatter.4
  148.6 31.4 reduce-scatter.2
where the time goes:
time: 189 us
  waiting for transfers between devices  108 us (57%)
  other arithmetic  25.1 us (13%)
  local copies, waits for them, and re-layouts  19.2 us (10%)
  matrix products  18.5 us (10%)
  between operations  13.2 us (7%)
  starting transfers between devices  4.77 us (3%)
    reduce_scatter x1, waiting for transfers between devices, local(): lax.psum_scatter(own_part, 'vox', scatter_dimension=0, tiled=True)  30.8 us
    reduce_scatter x1, waiting for transfers between devices, local(): lax.psum_scatter(next_part, 'vox', scatter_dimension=0, tiled=True)  30 us
    ppermute x2, waiting for transfers between devices, shifted(): return lax.ppermute(array, axis, pairs)  24.5 us
    all_gather x1, waiting for transfers between devices, local(): own_panel = lax.all_gather(probes, 'vox', axis=0, tiled=True)  21.1 us
    scatter-add x4, other arithmetic, local(): partial_value.at[pattern[:, slot]].add(back * scales[:, slot, None, None])  20.3 us
    dot_general x4, matrix products, local(): jnp.einsum('rab,rbk->rak', blocks[:, slot], picked, preferred_element_typ...  12.8 us
    mul x4, local copies, waits for them, and re-layouts, local(): back * scales[:, slot, None, None]  8.68 us
    dot_general x4, matrix products, local(): jnp.einsum('rab,rak->rbk', blocks[:, slot], weighted, preferred_element_t...  5.68 us
  transfers between devices with their start and end apart: 5, of which 4 were waited for; matrix products, arithmetic and copies ran while one was open for 1% of the time, Pallas kernels for 0%

commit v1 on v0

v1 whole, which is shorter than its diff:
```python
import functools

import jax
import jax.numpy as jnp
from jax import lax
from jax.experimental import pallas as pl
from jax.experimental.pallas import tpu as pltpu
from jax.sharding import PartitionSpec as P

MESH = pl.DeviceIdType.MESH


def kernel(
    groups, voxes, pattern, scale_exp, links, probes, blocks, noise, out,
    panels, chain, core_out, core_in, far_out, far_in,
    near_send, near_recv, y_send, y_recv, z_send, z_recv,
    pair_send, pair_recv, far_send, far_recv,
):
    rows_here, count, width = blocks.shape[0], blocks.shape[1], blocks.shape[2]
    held = probes.shape[0]
    ys = voxes // 2
    entries = rows_here * count
    cohort, grp, vox = lax.axis_index("cohort"), lax.axis_index("grp"), lax.axis_index("vox")
    y, core = vox // 2, lax.rem(vox, 2)
    before = lax.rem(grp + groups - 1, groups)
    after = lax.rem(grp + 1, groups)
    mate = (cohort, grp, 2 * y + 1 - core)

    def column(d):
        return lax.rem(y + d, ys)

    def device(group, d):
        return (cohort, group, 2 * column(d) + core)

    def shard(half, index):
        return panels.at[pl.ds((half * voxes + index) * held, held)]

    def remote(src, dst, send, recv, to):
        return pltpu.make_async_remote_copy(
            src_ref=src, dst_ref=dst, send_sem=send, recv_sem=recv, device_id=to, device_id_type=MESH
        )

    barrier = pltpu.get_barrier_semaphore()
    greeted = [mate] + [device(grp, d) for d in range(1, ys)]
    greeted += [device(group, d) for group in (before, after) for d in range(ys)]
    for other in greeted:
        pl.semaphore_signal(barrier, inc=1, device_id=other, device_id_type=MESH)
    pl.semaphore_wait(barrier, len(greeted))

    started = []

    def start(copy):
        copy.start()
        started.append(copy)

    for d in range(ys - 1, -1, -1):
        start(remote(probes, shard(1, vox), z_send.at[d], z_recv.at[d], device(before, d)))
    for d in range(1, ys):
        start(remote(probes, shard(0, vox), y_send.at[d - 1], y_recv.at[d - 1], device(grp, d)))
    start(remote(probes, shard(0, vox), near_send.at[0], near_recv.at[0], mate))
    panels[pl.ds(vox * held, held)] = probes[...]

    arrivals = []
    for d in range(1, ys):
        arrivals.append((0, d, y_send.at[d - 1], y_recv.at[d - 1]))
    for d in range(ys):
        arrivals.append((1, d, z_send.at[d], z_recv.at[d]))
    for place, (half, d, send, recv) in enumerate(arrivals):
        origin = 2 * lax.rem(y + ys - d, ys) + core
        slot = shard(half, origin)
        remote(slot, slot, send, recv, mate).wait_recv()
        start(remote(slot, slot, near_send.at[place + 1], near_recv.at[place + 1], mate))
    mates = [(0, 0)] + [(half, d) for half, d, _, _ in arrivals]
    for place, (half, d) in enumerate(mates):
        origin = 2 * lax.rem(y + ys - d, ys) + 1 - core
        slot = shard(half, origin)
        remote(slot, slot, near_send.at[place], near_recv.at[place], mate).wait_recv()

    def row(r, carry):
        scaled, picked = [], []
        for n in range(count):
            scale = lax.shift_left(jnp.int32(1), scale_exp[r * count + n] + 2).astype(jnp.float32) * 0.25
            scaled.append((blocks[r, n].astype(jnp.float32) * scale).astype(jnp.bfloat16))
            picked.append(panels[pattern[r * count + n]])
        left = jnp.concatenate(scaled, axis=1)
        forward = jnp.dot(left, jnp.concatenate(picked, axis=0), preferred_element_type=jnp.float32)
        weight = jnp.transpose(jnp.broadcast_to(noise[pl.ds(r, 1), :], (width, width)))
        weight = jnp.concatenate([weight] * (forward.shape[1] // width), axis=1)
        weighted = (weight * forward).astype(jnp.bfloat16)
        back = lax.dot_general(
            left, weighted, (((0,), (0,)), ((), ())), preferred_element_type=jnp.float32
        )
        for n in range(count):
            link = links[r * count + n]
            earlier = jnp.where(link >= 0, chain[jnp.maximum(link, 0)], 0.0)
            chain[r * count + n] = back[n * width : (n + 1) * width] + earlier
        return carry

    lax.fori_loop(0, rows_here, row, 0)

    def total(half, index, k):
        link = links[entries + (half * voxes + index) * held + k]
        return jnp.where(link >= 0, chain[jnp.maximum(link, 0)], 0.0)

    order = [(1, d) for d in range(ys - 1, -1, -1)] + [(0, d) for d in range(ys - 1, -1, -1)]
    for half, d in order:
        place = half * ys + d
        for k in range(held):
            core_out[place, k] = total(half, 2 * column(d) + 1 - core, k)
        start(remote(core_out.at[place], core_in.at[place], pair_send.at[place], pair_recv.at[place], mate))
    for half, d in order:
        place = half * ys + d
        remote(core_out.at[place], core_in.at[place], pair_send.at[place], pair_recv.at[place], mate).wait_recv()
        for k in range(held):
            both = total(half, 2 * column(d) + core, k) + core_in[place, k]
            if half == 0 and d == 0:
                out[k] = both
            else:
                far_out[place - 1, k] = both.astype(jnp.bfloat16)
        if half == 1 or d > 0:
            to = device(after if half else grp, d)
            start(remote(far_out.at[place - 1], far_in.at[place - 1], far_send.at[place - 1], far_recv.at[place - 1], to))
    for half, d in order:
        place = half * ys + d - 1
        if place >= 0:
            remote(far_out.at[place], far_in.at[place], far_send.at[place], far_recv.at[place], mate).wait_recv()
            for k in range(held):
                out[k] += far_in[place, k].astype(jnp.float32)
    for copy in started:
        copy.wait_send()


def solution(mesh):
    groups, voxes = mesh.shape["grp"], mesh.shape["vox"]

    def local(probes, blocks, pattern, scale_exp, noise):
        rows_here, count, width, _ = blocks.shape
        cols = probes.shape[1]
        held = probes.shape[0] // width
        entries = rows_here * count
        ys = voxes // 2
        flat = pattern.reshape(entries)
        numbers = jnp.arange(entries, dtype=jnp.int32)
        wanted = jnp.concatenate([flat, jnp.arange(2 * voxes * held, dtype=jnp.int32)])
        limit = jnp.concatenate([numbers, jnp.full((2 * voxes * held,), entries, jnp.int32)])
        match = (wanted[:, None] == flat[None, :]) & (numbers[None, :] < limit[:, None])
        links = jnp.max(jnp.where(match, numbers[None, :], -1), axis=1)
        smem = pl.BlockSpec(memory_space=pltpu.SMEM)
        vmem = pl.BlockSpec(memory_space=pltpu.VMEM)
        dma = pltpu.SemaphoreType.DMA
        result = pl.pallas_call(
            functools.partial(kernel, groups, voxes),
            out_shape=jax.ShapeDtypeStruct((held, width, cols), jnp.float32),
            in_specs=[smem] * 3 + [vmem] * 3,
            out_specs=vmem,
            scratch_shapes=[
                pltpu.VMEM((2 * voxes * held, width, cols), jnp.bfloat16),
                pltpu.VMEM((entries, width, cols), jnp.float32),
                pltpu.VMEM((2 * ys, held, width, cols), jnp.float32),
                pltpu.VMEM((2 * ys, held, width, cols), jnp.float32),
                pltpu.VMEM((2 * ys - 1, held, width, cols), jnp.bfloat16),
                pltpu.VMEM((2 * ys - 1, held, width, cols), jnp.bfloat16),
                dma((2 * ys,)), dma((2 * ys,)),
                dma((max(ys - 1, 1),)), dma((max(ys - 1, 1),)),
                dma((ys,)), dma((ys,)),
                dma((2 * ys,)), dma((2 * ys,)),
                dma((2 * ys - 1,)), dma((2 * ys - 1,)),
            ],
            compiler_params=pltpu.CompilerParams(
                collective_id=0, has_side_effects=True, vmem_limit_bytes=56 * 1024 * 1024
            ),
        )(flat, scale_exp.reshape(entries), links, probes.reshape(held, width, cols), blocks, noise)
        return result.reshape(held * width, cols)

    in_specs = (
        P(("cohort", "grp", "vox"), None),
        P(("cohort", "grp", "vox"), None, None, None),
        P(("cohort", "grp", "vox"), None),
        P(("cohort", "grp", "vox"), None),
        P(("cohort", "grp", "vox"), None),
    )
    out_specs = P(("cohort", "grp", "vox"), None)
    return jax.shard_map(local, mesh=mesh, in_specs=in_specs, out_specs=out_specs, check_vma=False)
```

time: 189 us -> 52.2 us (0.28)
  waiting for transfers between devices: 108 us -> 0 us
  Pallas kernels: 0 us -> 46.4 us
  other arithmetic: 25.1 us -> 1.32 us
  matrix products: 18.5 us -> 0 us
  local copies, waits for them, and re-layouts: 19.2 us -> 4.16 us
  between operations: 13.2 us -> 0.02 us
  starting transfers between devices: 4.77 us -> 0 us
    reduce_scatter x2 -> x0, waiting for transfers between devices: 60.7 us -> none  [the longest x1 30.8 us: local(): lax.psum_scatter(own_part, 'vox', scatter_dimension=0, tiled=True)]
    pallas_call x0 -> x1, Pallas kernels: none -> 46.4 us  [local(): pl.pallas_call(functools.partial(kernel, groups, voxes), out_shape=jax.Sh...]
    ppermute x2 -> x0, waiting for transfers between devices: 24.5 us -> none  [shifted(): return lax.ppermute(array, axis, pairs)]
    all_gather x1 -> x0, waiting for transfers between devices: 21.1 us -> none  [local(): own_panel = lax.all_gather(probes, 'vox', axis=0, tiled=True)]
    scatter-add x4 -> x0, other arithmetic: 20.3 us -> none  [local(): partial_value.at[pattern[:, slot]].add(back * scales[:, slot, None, None])]
    dot_general x8 -> x0, matrix products: 18.5 us -> none  [the longest x4 12.8 us: local(): jnp.einsum('rab,rbk->rak', blocks[:, slot], picked, preferred_element_typ...]
    mul x5 -> x0, local copies, waits for them, and re-layouts: 8.68 us -> none  [the longest x4 8.68 us: local(): back * scales[:, slot, None, None]]
    ppermute x2 -> x0, starting transfers between devices: 4.69 us -> none  [shifted(): return lax.ppermute(array, axis, pairs)]
  transfers between devices with their start and end apart: 5 -> 0, of which waited for: 4 -> 0; matrix products, arithmetic and copies ran while one was open for 1% -> 0% of each run, Pallas kernels for 0% -> 0%
where the time goes in v1:
time: 52.2 us; the launch traced here: 52 us
  Pallas kernels  46.4 us (89%)
  local copies, waits for them, and re-layouts  4.16 us (8%)
  other arithmetic  1.32 us (3%)
    pallas_call x1, Pallas kernels, local(): pl.pallas_call(functools.partial(kernel, groups, voxes), out_shape=jax.Sh...  46.4 us
    unnamed x5, local copies, waits for them, and re-layouts  3.39 us
    reduce_max x1, other arithmetic, local(): links = jnp.max(jnp.where(match, numbers[None, :], -1), axis=1)  1.25 us

profile of v1, /device:TPU:0, one launch (start us, length us, event | category | flops | bytes accessed | tf_op | source)
XLA Modules:
  0.0 52.0 jit_solution(3695463458676866405)
XLA Ops:
  0.0 0.8 %copy.10 = s32[16,4]{1,0:T(8,128)S(1)} copy(s32[16,4]{0,1:T(4,128)} %param.7) | data formatting | bytes 512 | tf_op args[2]
  0.8 0.1 reshape.15.pattern
  0.8 0.0 copy-start
  0.9 0.1 pad_add_fusion
  0.9 1.2 %select_reduce_fusion.links = s32[96]{0:T(128)} fusion(s32[96]{0:T(128)} %constant.1.clone.1, s32[96]{0:T(128)S(1)} %pad_add_fusion, s32[64]{0:T(128)S(1)} %reshape.15.pattern), kind=kLoop, calls=%fused_computation | loop fusion | flops 30624 | bytes 1408 | tf_op jit(solution)/shard_map/reduce_max | solution.py:147
  2.2 0.8 %copy.11 = s32[16,4]{1,0:T(8,128)S(1)} copy(s32[16,4]{0,1:T(4,128)} %param.8) | data formatting | bytes 512 | tf_op args[3]
  2.9 0.7 %reshape.16.scale_exp = s32[64]{0:T(128)} reshape(s32[16,4]{1,0:T(8,128)S(1)} %copy.11) | data formatting | bytes 512 | tf_op jit(solution)/shard_map/reshape | solution.py:172
  3.6 0.0 copy-done
  3.6 46.4 %shard_map.55 = f32[4,128,256]{2,1,0:T(8,128)} custom-call(s32[64]{0:T(128)} %copy-done, s32[64]{0:T(128)} %reshape.16.scale_exp, s32[96]{0:T(128)} %select_reduce_fusion.links, bf16[4,128,256]{2,1,0:T(8,128)(2,1)} %bitcast.3, bf16[16,4,128,128]{3,2,1,0:T(8,128)(2,1)} %blocks.1, f32[16,128]{1,0:T(8,128)} %noise.1), custom_call_target="tpu_custom_call" | custom-call | tf_op jit(solution)/shard_map/pallas_call | solution.py:151
  50.1 1.9 %copy.13 = f32[512,256]{1,0:T(8,128)} copy(f32[512,256]{1,0:T(8,128)} %bitcast.2) | data formatting | bytes 1048576
  (1 shorter events, 0.0 us)
Async XLA Ops:
  0.8 2.8 %copy-start = (s32[64]{0:T(128)}, s32[64]{0:T(128)S(1)}, u32[]{:S(2)}) copy-start(s32[64]{0:T(128)S(1)} %reshape.15.pattern) | copy-start | bytes 772

commit v2 on v0

v2 whole, which is shorter than its diff:
```python
import functools

import jax
import jax.numpy as jnp
from jax import lax
from jax.experimental import pallas as pl
from jax.experimental.pallas import tpu as pltpu
from jax.sharding import PartitionSpec as P

MESH = pl.DeviceIdType.MESH


def kernel(
    groups, voxes, scale_exp, pattern, probes, blocks, noise, out,
    panels, split, scaled, weights, chain, tables, other_pattern, other_noise, numbers,
    pair_out, pair_in, far_out, far_in,
    probe_send, probe_recv, mate_send, mate_recv, far_send, far_recv, local_sem,
):
    rows_here, count, width = blocks.shape[0], blocks.shape[1], blocks.shape[2]
    held = probes.shape[0]
    part = probes.shape[2] // 2
    ys = voxes // 2
    entries = rows_here * count
    cohort, grp, vox = lax.axis_index("cohort"), lax.axis_index("grp"), lax.axis_index("vox")
    y, core = vox // 2, lax.rem(vox, 2)
    before = lax.rem(grp + groups - 1, groups)
    after = lax.rem(grp + 1, groups)
    not_first, not_last = grp > 0, grp < groups - 1
    cores = (core, 1 - core)
    mate = (cohort, grp, 2 * y + 1 - core)

    def vox_at(d, q):
        return 2 * lax.rem(y + ys + d, ys) + cores[q]

    def device(group, d, q):
        return (cohort, group, vox_at(d, q))

    def shard(half, index):
        return panels.at[pl.ds((half * voxes + index) * held, held)]

    def remote(src, dst, send, recv, to):
        return pltpu.make_async_remote_copy(
            src_ref=src, dst_ref=dst, send_sem=send, recv_sem=recv, device_id=to, device_id_type=MESH
        )

    def when(condition, act):
        if condition is None:
            act()
        else:
            pl.when(condition)(act)

    places = [(1, d, q) for d in range(ys - 1, -1, -1) for q in (0, 1)]
    places += [(0, d, q) for d in range(ys - 1, 0, -1) for q in (0, 1)]

    barrier = pltpu.get_barrier_semaphore()
    greeted = [(None, mate)] + [(None, device(grp, d, q)) for d in range(1, ys) for q in (0, 1)]
    greeted += [(not_first, device(before, d, q)) for d in range(ys) for q in (0, 1)]
    greeted += [(not_last, device(after, d, q)) for d in range(ys) for q in (0, 1)]
    for condition, one in greeted:
        when(condition, functools.partial(
            pl.semaphore_signal, barrier, inc=1, device_id=one, device_id_type=MESH
        ))
    for j in range(2):
        split[j] = probes[:, :, j * part : (j + 1) * part]
    sides = not_first.astype(jnp.int32) + not_last.astype(jnp.int32)
    pl.semaphore_wait(barrier, 2 * ys - 1 + 2 * ys * sides)

    started = []

    def start(copy, condition=None):
        when(condition, copy.start)
        started.append((condition, copy))

    for place, (half, d, q) in enumerate(places):
        to = device(before if half else grp, d, q)
        copy = remote(split.at[cores[q]], shard(half, vox), probe_send.at[place], probe_recv.at[place], to)
        start(copy, not_first if half else None)
    start(remote(split.at[cores[1]], shard(0, vox), mate_send.at[0], mate_recv.at[0], mate))
    start(remote(pattern, other_pattern, mate_send.at[1], mate_recv.at[1], mate))
    start(remote(noise, other_noise, mate_send.at[2], mate_recv.at[2], mate))
    panels[pl.ds(vox * held, held)] = split[core]

    def prepare(r, carry):
        for n in range(count):
            scale = lax.shift_left(jnp.int32(1), scale_exp[n, r] + 2).astype(jnp.float32) * 0.25
            scaled[r, :, n * width : (n + 1) * width] = (
                blocks[r, n].astype(jnp.float32) * scale
            ).astype(jnp.bfloat16)
        return carry

    lax.fori_loop(0, rows_here, prepare, 0, unroll=2)
    start(remote(
        scaled.at[pl.ds(0, rows_here)], scaled.at[pl.ds(rows_here, rows_here)],
        mate_send.at[3], mate_recv.at[3], mate,
    ))

    def widen(ref, base):
        def one(r, carry):
            weights[base + r] = jnp.transpose(jnp.broadcast_to(ref[pl.ds(r, 1), :], (part, width)))
            return carry

        lax.fori_loop(0, rows_here, one, 0, unroll=2)

    widen(noise, 0)
    remote(pattern, other_pattern, mate_send.at[1], mate_recv.at[1], mate).wait_recv()
    remote(noise, other_noise, mate_send.at[2], mate_recv.at[2], mate).wait_recv()
    widen(other_noise, rows_here)

    both = 2 * entries
    columns = jnp.concatenate([ref[n : n + 1, :] for ref in (pattern, other_pattern) for n in range(count)], axis=1)
    square = jnp.broadcast_to(columns, (both, both))
    turned = jnp.transpose(square)
    row_id = lax.broadcasted_iota(jnp.int32, (both, both), 0)
    lane_id = lax.broadcasted_iota(jnp.int32, (both, both), 1)

    def turn(place):
        second = (place >= entries).astype(jnp.int32)
        within = place - second * entries
        n = sum((within >= m * rows_here).astype(jnp.int32) for m in range(1, count))
        return second * entries + (within - n * rows_here) * count + n

    row_turn, lane_turn = turn(row_id), turn(lane_id)
    tables[0:1] = jnp.max(
        jnp.where((turned == square) & (row_turn < lane_turn), row_turn, -1), axis=0, keepdims=True
    )
    tables[1:2] = jnp.max(jnp.where(turned == lane_id, row_turn, -1), axis=0, keepdims=True)
    tables[2:3] = columns
    tables[3:8] = jnp.zeros((5, both), jnp.int32)
    to_scalars = pltpu.make_async_copy(tables, numbers, local_sem)
    to_scalars.start()
    to_scalars.wait()

    slot = shard(0, vox_at(0, 1))
    remote(slot, slot, mate_send.at[0], mate_recv.at[0], mate).wait_recv()
    slot = scaled.at[pl.ds(rows_here, rows_here)]
    remote(slot, slot, mate_send.at[3], mate_recv.at[3], mate).wait_recv()
    for place, (half, d, q) in enumerate(places):
        slot = shard(half, vox_at(-d, q))
        copy = remote(slot, slot, probe_send.at[place], probe_recv.at[place], mate)
        when(not_last if half else None, copy.wait_recv)

    def row(r, carry):
        left = scaled[r]
        first = lax.div(r, rows_here) * entries + lax.rem(r, rows_here)
        numbered = [first + n * rows_here for n in range(count)]
        picked = jnp.concatenate([panels[numbers[2, i]] for i in numbered], axis=0)
        forward = jnp.dot(left, picked, preferred_element_type=jnp.float32)
        weighted = (weights[r] * forward).astype(jnp.bfloat16)
        back = lax.dot_general(
            left, weighted, (((0,), (0,)), ((), ())), preferred_element_type=jnp.float32
        )
        for n in range(count):
            link = numbers[0, numbered[n]]
            earlier = jnp.where(link >= 0, chain[jnp.maximum(link, 0)], 0.0)
            chain[r * count + n] = back[n * width : (n + 1) * width] + earlier
        return carry

    lax.fori_loop(0, 2 * rows_here, row, 0, unroll=4)

    def total(half, index, k):
        link = numbers[1, (half * voxes + index) * held + k]
        return jnp.where(link >= 0, chain[jnp.maximum(link, 0)], 0.0)

    for place, (half, d, q) in enumerate(places):
        for k in range(held):
            far_out[place, k] = total(half, vox_at(d, q), k).astype(jnp.bfloat16)
        to = device(after if half else grp, d, q)
        copy = remote(far_out.at[place], far_in.at[place], far_send.at[place], far_recv.at[place], to)
        start(copy, not_last if half else None)
    for k in range(held):
        pair_out[k] = total(0, vox_at(0, 1), k)
    start(remote(pair_out, pair_in, mate_send.at[4], mate_recv.at[4], mate))
    remote(pair_out, pair_in, mate_send.at[4], mate_recv.at[4], mate).wait_recv()
    for place, (half, d, q) in enumerate(places):
        copy = remote(far_out.at[place], far_in.at[place], far_send.at[place], far_recv.at[place], mate)
        when(not_first if half else None, copy.wait_recv)
    for k in range(held):
        sums = [total(0, vox, k), pair_in[k]]
        for place, (half, _, q) in enumerate(places):
            arrived = far_in[place, k].astype(jnp.float32)
            sums[q] = sums[q] + (jnp.where(not_first, arrived, 0.0) if half else arrived)
        out[core, k] = sums[0]
        out[1 - core, k] = sums[1]
    for condition, copy in started:
        when(condition, copy.wait_send)


def solution(mesh):
    groups, voxes = mesh.shape["grp"], mesh.shape["vox"]

    def local(probes, blocks, pattern, scale_exp, noise):
        rows_here, count, width, _ = blocks.shape
        cols = probes.shape[1]
        part = cols // 2
        held = probes.shape[0] // width
        entries = rows_here * count
        ys = voxes // 2
        apart = 4 * ys - 2
        smem = pl.BlockSpec(memory_space=pltpu.SMEM)
        vmem = pl.BlockSpec(memory_space=pltpu.VMEM)
        dma = pltpu.SemaphoreType.DMA
        result = pl.pallas_call(
            functools.partial(kernel, groups, voxes),
            out_shape=jax.ShapeDtypeStruct((2, held, width, part), jnp.float32),
            in_specs=[smem] + [vmem] * 4,
            out_specs=vmem,
            scratch_shapes=[
                pltpu.VMEM((2 * voxes * held, width, part), jnp.bfloat16),
                pltpu.VMEM((2, held, width, part), jnp.bfloat16),
                pltpu.VMEM((2 * rows_here, width, count * width), jnp.bfloat16),
                pltpu.VMEM((2 * rows_here, width, part), jnp.float32),
                pltpu.VMEM((2 * entries, width, part), jnp.float32),
                pltpu.VMEM((8, 2 * entries), jnp.int32),
                pltpu.VMEM((count, rows_here), jnp.int32),
                pltpu.VMEM(noise.shape, jnp.float32),
                pltpu.SMEM((8, 2 * entries), jnp.int32),
                pltpu.VMEM((held, width, part), jnp.float32),
                pltpu.VMEM((held, width, part), jnp.float32),
                pltpu.VMEM((apart, held, width, part), jnp.bfloat16),
                pltpu.VMEM((apart, held, width, part), jnp.bfloat16),
                dma((apart,)), dma((apart,)),
                dma((5,)), dma((5,)),
                dma((apart,)), dma((apart,)),
                dma,
            ],
            compiler_params=pltpu.CompilerParams(
                collective_id=0, has_side_effects=True, vmem_limit_bytes=56 * 1024 * 1024
            ),
        )(scale_exp.T, pattern.T, probes.reshape(held, width, cols), blocks, noise)
        halves = result.reshape(2, held * width, part)
        return jnp.concatenate([halves[0], halves[1]], axis=1)

    in_specs = (
        P(("cohort", "grp", "vox"), None),
        P(("cohort", "grp", "vox"), None, None, None),
        P(("cohort", "grp", "vox"), None),
        P(("cohort", "grp", "vox"), None),
        P(("cohort", "grp", "vox"), None),
    )
    out_specs = P(("cohort", "grp", "vox"), None)
    return jax.shard_map(local, mesh=mesh, in_specs=in_specs, out_specs=out_specs, check_vma=False)
```

time: 189 us -> 39.7 us (0.21)
  waiting for transfers between devices: 108 us -> 0 us
  Pallas kernels: 0 us -> 37.7 us
  other arithmetic: 25.1 us -> 0.83 us
  matrix products: 18.5 us -> 0 us
  local copies, waits for them, and re-layouts: 19.2 us -> 1.07 us
  between operations: 13.2 us -> 0.01 us
  starting transfers between devices: 4.77 us -> 0 us
    reduce_scatter x2 -> x0, waiting for transfers between devices: 60.7 us -> none  [the longest x1 30.8 us: local(): lax.psum_scatter(own_part, 'vox', scatter_dimension=0, tiled=True)]
    pallas_call x0 -> x1, Pallas kernels: none -> 37.7 us  [local(): pl.pallas_call(functools.partial(kernel, groups, voxes), out_shape=jax.Sh...]
    ppermute x2 -> x0, waiting for transfers between devices: 24.5 us -> none  [shifted(): return lax.ppermute(array, axis, pairs)]
    all_gather x1 -> x0, waiting for transfers between devices: 21.1 us -> none  [local(): own_panel = lax.all_gather(probes, 'vox', axis=0, tiled=True)]
    scatter-add x4 -> x0, other arithmetic: 20.3 us -> none  [local(): partial_value.at[pattern[:, slot]].add(back * scales[:, slot, None, None])]
    dot_general x8 -> x0, matrix products: 18.5 us -> none  [the longest x4 12.8 us: local(): jnp.einsum('rab,rbk->rak', blocks[:, slot], picked, preferred_element_typ...]
    mul x5 -> x0, local copies, waits for them, and re-layouts: 8.68 us -> none  [the longest x4 8.68 us: local(): back * scales[:, slot, None, None]]
    ppermute x2 -> x0, starting transfers between devices: 4.69 us -> none  [shifted(): return lax.ppermute(array, axis, pairs)]
  transfers between devices with their start and end apart: 5 -> 0, of which waited for: 4 -> 0; matrix products, arithmetic and copies ran while one was open for 1% -> 0% of each run, Pallas kernels for 0% -> 0%
where the time goes in v2:
time: 39.7 us; the launch traced here: 39.6 us
  Pallas kernels  37.7 us (95%)
  local copies, waits for them, and re-layouts  1.07 us (3%)
  other arithmetic  0.83 us (2%)
    pallas_call x1, Pallas kernels, local(): pl.pallas_call(functools.partial(kernel, groups, voxes), out_shape=jax.Sh...  37.7 us
    slice x1, local copies, waits for them, and re-layouts, local(): return jnp.concatenate([halves[0], halves[1]], axis=1)  1.07 us
    concatenate x1, other arithmetic, local(): return jnp.concatenate([halves[0], halves[1]], axis=1)  0.83 us

profile of v2, /device:TPU:0, one launch (start us, length us, event | category | flops | bytes accessed | tf_op | source)
XLA Modules:
  0.0 39.6 jit_solution(2039838386714988265)
XLA Ops:
  0.0 37.7 %shard_map.55 = f32[2,4,128,128]{3,2,1,0:T(8,128)} custom-call(s32[4,16]{1,0:T(4,128)} %bitcast.8, s32[4,16]{1,0:T(4,128)} %bitcast.9, bf16[4,128,256]{2,1,0:T(8,128)(2,1)} %bitcast.7, bf16[16,4,128,128]{3,2,1,0:T(8,128)(2,1)} %blocks.1, f32[16,128]{1,0:T(8,128)} %noise.1), custom_call_target="tpu_custom_call" | custom-call | tf_op jit(solution)/shard_map/pallas_call | solution.py:202
  37.7 1.1 %fusion = (f32[1,4,128,128]{3,2,1,0:T(8,128)S(1)}, f32[1,4,128,128]{3,2,1,0:T(8,128)S(1)}) fusion(f32[2,4,128,128]{3,2,1,0:T(8,128)} %shard_map.55), kind=kLoop, calls=%fused_computation.1 | loop fusion | bytes 1048576 | tf_op jit(solution)/shard_map/slice | solution.py:231
  38.7 0.8 %pad_maximum_fusion = f32[512,256]{1,0:T(8,128)} fusion(f32[512,128]{1,0:T(8,128)S(1)} %bitcast.6, f32[512,128]{1,0:T(8,128)S(1)} %bitcast.5), kind=kLoop, calls=%fused_computation | loop fusion | flops 131072 | bytes 1048576 | tf_op jit(solution)/shard_map/concatenate | solution.py:231
